TPU v7x, 32 devices: a whole 2x2x4 slice. The times are simulated.
32 devices in a mesh: runs: 2 (over x), area: 16 (over z, y, core).
Axes of the slice: x: 2, y: 2, z: 4, core: 2. Of those that a mesh axis runs over, the one named last changes fastest.
Arguments:
- history: bfloat16 [4, 32, 16384], P(None, 'runs', 'area'), parts along dimension 1, may hold values from 0 to 1
- drive: bfloat16 [32, 16384], P('runs', 'area'), parts along dimension 0, may hold values from -6 to 6
- leak: float32 [32768], P(('runs', 'area')), parts along dimension 0, may hold values from 0.1 to 0.9
- inhibition: float32 [16], P('runs'), parts along dimension 0, may hold values from 0.5 to 4
- section: int32 [16], replicated, may hold values from 0 to 7, never falling along the last dimension, each value on 1 to 6 neighbouring positions
- link_source: int32 [768, 1], P('area'), may hold values from 0 to 15; in each aligned block of 48 rows (0 to 47, 48 to 95, ...) at most 3 rows name the same one
- link_block: int32 [768], P('area'), may hold values from 0 to 3
- link_target: int32 [768], P('area'), may hold values from 0 to 3
- link_delay: int32 [768], P('area'), may hold values from 2 to 4
- remote_weight: bfloat16 [1536, 256, 256], P(('runs', 'area')), parts along dimension 0, may hold values from -0.375 to 0.375
- local_block: int32 [256], P('area'), may hold values from 0 to 3
- local_target: int32 [256], P('area'), may hold values from 0 to 3
- local_delay: int32 [256], P('area'), may hold values from 1 to 4
- local_weight: bfloat16 [512, 256, 256], P(('runs', 'area')), parts along dimension 0, may hold values from -0.375 to 0.375
Outputs:
- rates: bfloat16 [32, 16384], P('runs', 'area'), parts along dimension 0
There are 2 independent parts, one for each index of `runs`. A program takes and returns all parts, laid end to end along the dimension named above; an argument that names none is the same for every part. Nothing has to cross between parts.
Inputs may be any that keep to these rules, and one draw needn't show every extreme that they name: `section`: Nondecreasing; every area covers 1 to 6 consecutive indices, and some area covers exactly 6. `link_source`: among the 48 remote tiles of one index of area, no index of area is named more than 3 times, a bound that some block reaches.
All inputs are finite; a program needn't handle non-finite values.
Results may differ from a plain program's by a relative error of at most 0.005.
Values may be sent and summed in bfloat16 or wider, within the bound.
A program may use at most 128 MiB of HBM per device.

v0:
```python
import jax
import jax.numpy as jnp
from jax import lax
from jax.sharding import PartitionSpec as P

STEPS = 6


def local(
    history,
    drive,
    leak,
    inhibition,
    section,
    link_source,
    link_block,
    link_target,
    link_delay,
    remote_weight,
    local_block,
    local_target,
    local_delay,
    local_weight,
):
    delay_depth, trials, row_width = history.shape
    pop_size = remote_weight.shape[1]
    blocks = row_width // pop_size
    link_count = link_block.shape[0]
    devices = lax.axis_size("area")
    capacity = max(2, (link_count + devices - 1) // devices)
    slot_total = devices * capacity
    area_total = inhibition.shape[0]
    state_rows = (
        history.reshape(delay_depth, trials, blocks, pop_size)
        .transpose(0, 2, 1, 3)
        .reshape(delay_depth * blocks, trials, pop_size)
    )
    source = link_source[:, 0]
    positions = jnp.arange(link_count, dtype=jnp.int32)
    earlier = (source[:, None] == source[None, :]) & (positions[None, :] < positions[:, None])
    slot_rank = jnp.sum(earlier.astype(jnp.int32), axis=1)
    slot_index = source * capacity + slot_rank
    slot_table = slot_index[:, None] == jnp.arange(slot_total, dtype=jnp.int32)[None, :]
    slot_used = jnp.any(slot_table, axis=0)
    want_block = jnp.sum(jnp.where(slot_table, link_block[:, None], 0), axis=0)
    want_delay = jnp.where(
        slot_used, jnp.sum(jnp.where(slot_table, link_delay[:, None], 0), axis=0), delay_depth
    )
    asked_block, asked_delay = (
        lax.all_to_all(
            want_block.reshape(devices, capacity), "area", split_axis=0, concat_axis=0, tiled=True
        ),
        lax.all_to_all(
            want_delay.reshape(devices, capacity), "area", split_axis=0, concat_axis=0, tiled=True
        ),
    )
    asked_block = asked_block.reshape(slot_total)
    asked_delay = asked_delay.reshape(slot_total)
    target_onehot = (link_target[None, :] == jnp.arange(blocks, dtype=jnp.int32)[:, None]).astype(
        jnp.float32
    )
    local_onehot = (local_target[None, :] == jnp.arange(blocks, dtype=jnp.int32)[:, None]).astype(
        jnp.float32
    )
    local_index = (local_delay - 1) * blocks + local_block
    leak_rows = leak.reshape(blocks, pop_size)[:, None, :]
    drive_blocks = drive.astype(jnp.float32).reshape(trials, blocks, pop_size).transpose(1, 0, 2)
    my_index = lax.axis_index("area")
    my_area = lax.dynamic_slice_in_dim(section, my_index, 1, 0)[0]
    area_mask = jnp.arange(area_total, dtype=jnp.int32) == my_area
    area_count = jnp.sum((section == my_area).astype(jnp.float32)) * row_width
    inhibit = jnp.sum(jnp.where(area_mask, inhibition, 0.0))
    fresh = state_rows[:blocks]
    for step_index in range(STEPS):
        outgoing = jnp.take(state_rows, (asked_delay - 1) * blocks + asked_block, axis=0).reshape(
            devices, capacity, trials, pop_size
        )
        received = lax.all_to_all(
            outgoing, "area", split_axis=0, concat_axis=0, tiled=True
        ).reshape(slot_total, trials, pop_size)
        remote_in = jnp.take(received, slot_index, axis=0)
        previous = state_rows[:blocks].astype(jnp.float32)
        own_sum = jnp.sum(previous, axis=(0, 2))
        area_table = jnp.where(area_mask[:, None], own_sum[None, :], 0.0)
        summed = lax.psum(area_table, "area")
        total_mine = jnp.sum(jnp.where(area_mask[:, None], summed, 0.0), axis=0)
        mean_now = total_mine / area_count
        local_in = jnp.take(state_rows, local_index, axis=0)
        local_terms = jnp.einsum(
            "ltp,lpq->ltq", local_in, local_weight, preferred_element_type=jnp.float32
        )
        remote_terms = jnp.einsum(
            "ltp,lpq->ltq", remote_in, remote_weight, preferred_element_type=jnp.float32
        )
        current = jnp.einsum(
            "bl,ltq->btq", target_onehot, remote_terms, precision=lax.Precision.HIGHEST
        )
        current = current + jnp.einsum(
            "bl,ltq->btq", local_onehot, local_terms, precision=lax.Precision.HIGHEST
        )
        driven = jax.nn.sigmoid(current + drive_blocks - inhibit * mean_now[None, :, None])
        fresh = ((1.0 - leak_rows) * previous + leak_rows * driven).astype(jnp.bfloat16)
        state_rows = jnp.concatenate([fresh, state_rows[:-blocks]], axis=0)
    return fresh.transpose(1, 0, 2).reshape(trials, row_width)


def solution(mesh):
    placed = (
        P(None, "runs", "area"),
        P("runs", "area"),
        P(("runs", "area")),
        P("runs"),
        P(),
        P("area", None),
        P("area"),
        P("area"),
        P("area"),
        P(("runs", "area"), None, None),
        P("area"),
        P("area"),
        P("area"),
        P(("runs", "area"), None, None),
    )
    return jax.shard_map(
        local, mesh=mesh, in_specs=placed, out_specs=P("runs", "area"), check_vma=False
    )
```

profile of v0, /device:TPU:1, one launch (start us, length us, event | category | flops | bytes accessed | tf_op | source)
XLA Modules:
  0.0 360.8 jit_solution(18329687779567038272)
XLA Ops:
  3.1 7.3 %all-to-all-start.1 = ((s32[16,1,3]{2,1,0:T(1,128)}), s32[16,1,3]{2,1,0:T(1,128)S(1)}, u32[]{:S(2)}, u32[]{:S(2)}) async-start(s32[16,1,3]{2,1,0:T(1,128)} %bitcast.6), calls=%async_computation.1 | async-start | bytes 16384 | tf_op jit(solution)/shard_map/all_to_all | solution.py:50
  12.2 1.3 dynamic_slice.3
  14.2 2.0 select_reduce_fusion.8
  17.8 29.2 %psum.42 = f32[8,16]{1,0:T(8,128)S(1)} all-reduce(f32[8,16]{1,0:T(8,128)S(1)} %broadcast_select_fusion.11), channel_id=1, replica_groups=mesh['runs'=2,'area'=16] {'area'}, use_global_device_ids=true, to_apply=%region_7.11 | all-reduce | flops 128 | bytes 1024 | tf_op jit(solution)/shard_map/psum | solution.py:85
  47.2 1.9 fusion.129
  49.8 8.0 %all-to-all-start = ((s32[16,1,3]{2,1,0:T(1,128)}), s32[16,1,3]{2,1,0:T(1,128)S(1)}, u32[]{:S(2)}, u32[]{:S(2)}) async-start(s32[16,1,3]{2,1,0:T(1,128)} %bitcast.5), calls=%async_computation | async-start | bytes 16384 | tf_op jit(solution)/shard_map/all_to_all | solution.py:53
  59.7 3.9 %all-to-all-done = s32[16,1,3]{2,1,0:T(1,128)S(1)} async-done(((s32[16,1,3]{2,1,0:T(1,128)}), s32[16,1,3]{2,1,0:T(1,128)S(1)}, u32[]{:S(2)}, u32[]{:S(2)}) %all-to-all-start) | async-done | bytes 224 | tf_op jit(solution)/shard_map/all_to_all | solution.py:53
  65.3 4.1 %all-to-all-start.2 = ((bf16[16,3,16,256]{3,2,1,0:T(8,128)(2,1)}), bf16[16,3,16,256]{3,2,1,0:T(8,128)(2,1)S(1)}, u32[]{:S(2)}, u32[]{:S(2)}) async-start(bf16[16,3,16,256]{3,2,1,0:T(8,128)(2,1)} %bitcast.8), calls=%async_computation.2 | async-start | bytes 786432 | tf_op jit(solution)/shard_map/all_to_all | solution.py:78
  70.4 1.0 fusion.88
  71.4 9.9 %all-to-all-done.2 = bf16[16,3,16,256]{3,2,1,0:T(8,128)(2,1)S(1)} async-done(((bf16[16,3,16,256]{3,2,1,0:T(8,128)(2,1)}), bf16[16,3,16,256]{3,2,1,0:T(8,128)(2,1)S(1)}, u32[]{:S(2)}, u32[]{:S(2)}) %all-to-all-start.2) | async-done | bytes 393248 | tf_op jit(solution)/shard_map/all_to_all | solution.py:78
  81.9 3.8 %fusion.70 = f32[48,16,256]{2,1,0:T(8,128)S(1)} fusion(bf16[48,256,256]{2,1,0:T(8,128)(2,1)} %param.29, bf16[48,16,256]{2,1,0:T(8,128)(2,1)S(1)} %gather_fusion.1, pred[48]{0:T(512)(128)(4,1)S(1)} %get-tuple-element.10), kind=kOutput, calls=%fused_computation.94 | convolution fusion | flops 100859904 | bytes 7471152 | tf_op jit(solution)/shard_map/ltp,lpq->ltq/dot_general | solution.py:92
  85.7 1.0 convert_reduce_fusion.4
  88.0 29.2 %psum.43 = f32[8,16]{1,0:T(8,128)S(1)} all-reduce(f32[8,16]{1,0:T(8,128)S(1)} %broadcast_select_fusion.10), channel_id=1, replica_groups=mesh['runs'=2,'area'=16] {'area'}, use_global_device_ids=true, to_apply=%region_11.15 | all-reduce | flops 128 | bytes 1024 | tf_op jit(solution)/shard_map/psum | solution.py:85
  118.1 6.0 %all-to-all-start.3 = ((bf16[16,3,16,256]{3,2,1,0:T(8,128)(2,1)}), bf16[16,3,16,256]{3,2,1,0:T(8,128)(2,1)S(1)}, u32[]{:S(2)}, u32[]{:S(2)}) async-start(bf16[16,3,16,256]{3,2,1,0:T(8,128)(2,1)} %bitcast.14), calls=%async_computation.3 | async-start | bytes 786432 | tf_op jit(solution)/shard_map/all_to_all | solution.py:78
  125.5 10.5 %all-to-all-done.3 = bf16[16,3,16,256]{3,2,1,0:T(8,128)(2,1)S(1)} async-done(((bf16[16,3,16,256]{3,2,1,0:T(8,128)(2,1)}), bf16[16,3,16,256]{3,2,1,0:T(8,128)(2,1)S(1)}, u32[]{:S(2)}, u32[]{:S(2)}) %all-to-all-start.3) | async-done | bytes 393248 | tf_op jit(solution)/shard_map/all_to_all | solution.py:78
  136.7 3.7 %fusion.68 = f32[48,16,256]{2,1,0:T(8,128)S(1)} fusion(bf16[48,256,256]{2,1,0:T(8,128)(2,1)} %param.29, bf16[48,16,256]{2,1,0:T(8,128)(2,1)S(1)} %gather_fusion.4, pred[48]{0:T(512)(128)(4,1)S(1)} %get-tuple-element.10), kind=kOutput, calls=%fused_computation.92 | convolution fusion | flops 100859904 | bytes 7471152 | tf_op jit(solution)/shard_map/ltp,lpq->ltq/dot_general | solution.py:92
  142.7 29.2 %psum.44 = f32[8,16]{1,0:T(8,128)S(1)} all-reduce(f32[8,16]{1,0:T(8,128)S(1)} %broadcast_select_fusion.9), channel_id=1, replica_groups=mesh['runs'=2,'area'=16] {'area'}, use_global_device_ids=true, to_apply=%region_14.18 | all-reduce | flops 128 | bytes 1024 | tf_op jit(solution)/shard_map/psum | solution.py:85
  172.9 6.0 %all-to-all-start.4 = ((bf16[16,3,16,256]{3,2,1,0:T(8,128)(2,1)}), bf16[16,3,16,256]{3,2,1,0:T(8,128)(2,1)S(1)}, u32[]{:S(2)}, u32[]{:S(2)}) async-start(bf16[16,3,16,256]{3,2,1,0:T(8,128)(2,1)} %bitcast.16), calls=%async_computation.4 | async-start | bytes 786432 | tf_op jit(solution)/shard_map/all_to_all | solution.py:78
  180.3 10.6 %all-to-all-done.4 = bf16[16,3,16,256]{3,2,1,0:T(8,128)(2,1)S(1)} async-done(((bf16[16,3,16,256]{3,2,1,0:T(8,128)(2,1)}), bf16[16,3,16,256]{3,2,1,0:T(8,128)(2,1)S(1)}, u32[]{:S(2)}, u32[]{:S(2)}) %all-to-all-start.4) | async-done | bytes 393248 | tf_op jit(solution)/shard_map/all_to_all | solution.py:78
  191.4 3.7 %fusion.66 = f32[48,16,256]{2,1,0:T(8,128)S(1)} fusion(bf16[48,256,256]{2,1,0:T(8,128)(2,1)} %param.29, bf16[48,16,256]{2,1,0:T(8,128)(2,1)S(1)} %gather_fusion.7, pred[48]{0:T(512)(128)(4,1)S(1)} %get-tuple-element.10), kind=kOutput, calls=%fused_computation.90 | convolution fusion | flops 100859904 | bytes 7471152 | tf_op jit(solution)/shard_map/ltp,lpq->ltq/dot_general | solution.py:92
  197.4 29.2 %psum.45 = f32[8,16]{1,0:T(8,128)S(1)} all-reduce(f32[8,16]{1,0:T(8,128)S(1)} %broadcast_select_fusion.8), channel_id=1, replica_groups=mesh['runs'=2,'area'=16] {'area'}, use_global_device_ids=true, to_apply=%region_17.21 | all-reduce | flops 128 | bytes 1024 | tf_op jit(solution)/shard_map/psum | solution.py:85
  227.6 6.0 %all-to-all-start.5 = ((bf16[16,3,16,256]{3,2,1,0:T(8,128)(2,1)}), bf16[16,3,16,256]{3,2,1,0:T(8,128)(2,1)S(1)}, u32[]{:S(2)}, u32[]{:S(2)}) async-start(bf16[16,3,16,256]{3,2,1,0:T(8,128)(2,1)} %bitcast.18), calls=%async_computation.5 | async-start | bytes 786432 | tf_op jit(solution)/shard_map/all_to_all | solution.py:78
  235.0 10.6 %all-to-all-done.5 = bf16[16,3,16,256]{3,2,1,0:T(8,128)(2,1)S(1)} async-done(((bf16[16,3,16,256]{3,2,1,0:T(8,128)(2,1)}), bf16[16,3,16,256]{3,2,1,0:T(8,128)(2,1)S(1)}, u32[]{:S(2)}, u32[]{:S(2)}) %all-to-all-start.5) | async-done | bytes 393248 | tf_op jit(solution)/shard_map/all_to_all | solution.py:78
  246.1 3.7 %fusion.64 = f32[48,16,256]{2,1,0:T(8,128)S(1)} fusion(bf16[48,256,256]{2,1,0:T(8,128)(2,1)} %param.29, bf16[48,16,256]{2,1,0:T(8,128)(2,1)S(1)} %gather_fusion.10, pred[48]{0:T(512)(128)(4,1)S(1)} %get-tuple-element.10), kind=kOutput, calls=%fused_computation.88 | convolution fusion | flops 100859904 | bytes 7471152 | tf_op jit(solution)/shard_map/ltp,lpq->ltq/dot_general | solution.py:92
  252.2 29.2 %psum.46 = f32[8,16]{1,0:T(8,128)S(1)} all-reduce(f32[8,16]{1,0:T(8,128)S(1)} %broadcast_select_fusion.7), channel_id=1, replica_groups=mesh['runs'=2,'area'=16] {'area'}, use_global_device_ids=true, to_apply=%region_20.24 | all-reduce | flops 128 | bytes 1024 | tf_op jit(solution)/shard_map/psum | solution.py:85
  282.3 6.0 %all-to-all-start.6 = ((bf16[16,3,16,256]{3,2,1,0:T(8,128)(2,1)}), bf16[16,3,16,256]{3,2,1,0:T(8,128)(2,1)S(1)}, u32[]{:S(2)}, u32[]{:S(2)}) async-start(bf16[16,3,16,256]{3,2,1,0:T(8,128)(2,1)} %bitcast.20), calls=%async_computation.6 | async-start | bytes 786432 | tf_op jit(solution)/shard_map/all_to_all | solution.py:78
  289.7 10.6 %all-to-all-done.6 = bf16[16,3,16,256]{3,2,1,0:T(8,128)(2,1)S(1)} async-done(((bf16[16,3,16,256]{3,2,1,0:T(8,128)(2,1)}), bf16[16,3,16,256]{3,2,1,0:T(8,128)(2,1)S(1)}, u32[]{:S(2)}, u32[]{:S(2)}) %all-to-all-start.6) | async-done | bytes 393248 | tf_op jit(solution)/shard_map/all_to_all | solution.py:78
  300.9 3.7 %fusion.62 = f32[48,16,256]{2,1,0:T(8,128)S(1)} fusion(bf16[48,256,256]{2,1,0:T(8,128)(2,1)} %param.29, bf16[48,16,256]{2,1,0:T(8,128)(2,1)S(1)} %gather_fusion.13, pred[48]{0:T(512)(128)(4,1)S(1)} %get-tuple-element.10), kind=kOutput, calls=%fused_computation.86 | convolution fusion | flops 100859904 | bytes 7471152 | tf_op jit(solution)/shard_map/ltp,lpq->ltq/dot_general | solution.py:92
  306.9 29.2 %psum.47 = f32[8,16]{1,0:T(8,128)S(1)} all-reduce(f32[8,16]{1,0:T(8,128)S(1)} %broadcast_select_fusion.6), channel_id=1, replica_groups=mesh['runs'=2,'area'=16] {'area'}, use_global_device_ids=true, to_apply=%region_23.27 | all-reduce | flops 128 | bytes 1024 | tf_op jit(solution)/shard_map/psum | solution.py:85
  337.1 6.0 %all-to-all-start.7 = ((bf16[16,3,16,256]{3,2,1,0:T(8,128)(2,1)}), bf16[16,3,16,256]{3,2,1,0:T(8,128)(2,1)S(1)}, u32[]{:S(2)}, u32[]{:S(2)}) async-start(bf16[16,3,16,256]{3,2,1,0:T(8,128)(2,1)} %bitcast.22), calls=%async_computation.7 | async-start | bytes 786432 | tf_op jit(solution)/shard_map/all_to_all | solution.py:78
  344.4 10.6 %all-to-all-done.7 = bf16[16,3,16,256]{3,2,1,0:T(8,128)(2,1)S(1)} async-done(((bf16[16,3,16,256]{3,2,1,0:T(8,128)(2,1)}), bf16[16,3,16,256]{3,2,1,0:T(8,128)(2,1)S(1)}, u32[]{:S(2)}, u32[]{:S(2)}) %all-to-all-start.7) | async-done | bytes 393248 | tf_op jit(solution)/shard_map/all_to_all | solution.py:78
  355.6 3.7 %fusion.60 = f32[48,16,256]{2,1,0:T(8,128)S(1)} fusion(bf16[48,256,256]{2,1,0:T(8,128)(2,1)} %param.29, bf16[48,16,256]{2,1,0:T(8,128)(2,1)S(1)} %gather_fusion.16, pred[48]{0:T(512)(128)(4,1)S(1)} %get-tuple-element.10), kind=kOutput, calls=%fused_computation.84 | convolution fusion | flops 100859904 | bytes 7471152 | tf_op jit(solution)/shard_map/ltp,lpq->ltq/dot_general | solution.py:92
  (107 shorter events, 38.9 us)
Async XLA Ops:
  0.0 70.0 %copy-start = (bf16[16,256,256]{2,1,0:T(8,128)(2,1)S(1)}, bf16[16,256,256]{2,1,0:T(8,128)(2,1)}, u32[]{:S(2)}) copy-start(bf16[16,256,256]{2,1,0:T(8,128)(2,1)} %param.33) | copy-start | bytes 6291460
  3.1 46.6 %all-to-all-start.1 = ((s32[16,1,3]{2,1,0:T(1,128)}), s32[16,1,3]{2,1,0:T(1,128)S(1)}, u32[]{:S(2)}, u32[]{:S(2)}) async-start(s32[16,1,3]{2,1,0:T(1,128)} %bitcast.6), calls=%async_computation.1 | async-start | bytes 16384 | tf_op jit(solution)/shard_map/all_to_all | solution.py:50
  49.8 13.9 %all-to-all-start = ((s32[16,1,3]{2,1,0:T(1,128)}), s32[16,1,3]{2,1,0:T(1,128)S(1)}, u32[]{:S(2)}, u32[]{:S(2)}) async-start(s32[16,1,3]{2,1,0:T(1,128)} %bitcast.5), calls=%async_computation | async-start | bytes 16384 | tf_op jit(solution)/shard_map/all_to_all | solution.py:53
  64.4 21.3 %copy-start.2 = (s32[48]{0:T(128)S(1)}, s32[48]{0:T(128)}, u32[]{:S(2)}) copy-start(s32[48]{0:T(128)} %param.27) | copy-start | bytes 580
  65.3 16.0 %all-to-all-start.2 = ((bf16[16,3,16,256]{3,2,1,0:T(8,128)(2,1)}), bf16[16,3,16,256]{3,2,1,0:T(8,128)(2,1)S(1)}, u32[]{:S(2)}, u32[]{:S(2)}) async-start(bf16[16,3,16,256]{3,2,1,0:T(8,128)(2,1)} %bitcast.8), calls=%async_computation.2 | async-start | bytes 786432 | tf_op jit(solution)/shard_map/all_to_all | solution.py:78
  81.9 43.2 %copy-start.1 = (s32[16]{0:T(128)S(1)}, s32[16]{0:T(128)}, u32[]{:S(2)}) copy-start(s32[16]{0:T(128)} %param.31) | copy-start | bytes 196
  118.1 17.9 %all-to-all-start.3 = ((bf16[16,3,16,256]{3,2,1,0:T(8,128)(2,1)}), bf16[16,3,16,256]{3,2,1,0:T(8,128)(2,1)S(1)}, u32[]{:S(2)}, u32[]{:S(2)}) async-start(bf16[16,3,16,256]{3,2,1,0:T(8,128)(2,1)} %bitcast.14), calls=%async_computation.3 | async-start | bytes 786432 | tf_op jit(solution)/shard_map/all_to_all | solution.py:78
  172.9 17.9 %all-to-all-start.4 = ((bf16[16,3,16,256]{3,2,1,0:T(8,128)(2,1)}), bf16[16,3,16,256]{3,2,1,0:T(8,128)(2,1)S(1)}, u32[]{:S(2)}, u32[]{:S(2)}) async-start(bf16[16,3,16,256]{3,2,1,0:T(8,128)(2,1)} %bitcast.16), calls=%async_computation.4 | async-start | bytes 786432 | tf_op jit(solution)/shard_map/all_to_all | solution.py:78
  227.6 17.9 %all-to-all-start.5 = ((bf16[16,3,16,256]{3,2,1,0:T(8,128)(2,1)}), bf16[16,3,16,256]{3,2,1,0:T(8,128)(2,1)S(1)}, u32[]{:S(2)}, u32[]{:S(2)}) async-start(bf16[16,3,16,256]{3,2,1,0:T(8,128)(2,1)} %bitcast.18), calls=%async_computation.5 | async-start | bytes 786432 | tf_op jit(solution)/shard_map/all_to_all | solution.py:78
  282.3 17.9 %all-to-all-start.6 = ((bf16[16,3,16,256]{3,2,1,0:T(8,128)(2,1)}), bf16[16,3,16,256]{3,2,1,0:T(8,128)(2,1)S(1)}, u32[]{:S(2)}, u32[]{:S(2)}) async-start(bf16[16,3,16,256]{3,2,1,0:T(8,128)(2,1)} %bitcast.20), calls=%async_computation.6 | async-start | bytes 786432 | tf_op jit(solution)/shard_map/all_to_all | solution.py:78
  337.1 17.9 %all-to-all-start.7 = ((bf16[16,3,16,256]{3,2,1,0:T(8,128)(2,1)}), bf16[16,3,16,256]{3,2,1,0:T(8,128)(2,1)S(1)}, u32[]{:S(2)}, u32[]{:S(2)}) async-start(bf16[16,3,16,256]{3,2,1,0:T(8,128)(2,1)} %bitcast.22), calls=%async_computation.7 | async-start | bytes 786432 | tf_op jit(solution)/shard_map/all_to_all | solution.py:78
where the time goes:
time: 363 us; the launch traced here: 361 us
  blocking collectives  175 us (48%)
  waiting for transfers between devices  66.6 us (18%)
  starting transfers between devices  49.2 us (14%)
  matrix products  33.8 us (9%)
  other arithmetic  18.7 us (5%)
  local copies, waits for them, and re-layouts  16.2 us (4%)
    psum x6, blocking collectives, local(): summed = lax.psum(area_table, 'area')  175 us
    all_to_all x6, waiting for transfers between devices, local(): lax.all_to_all(outgoing, 'area', split_axis=0, concat_axis=0, tiled=True)  62.6 us
    all_to_all x6, starting transfers between devices, local(): lax.all_to_all(outgoing, 'area', split_axis=0, concat_axis=0, tiled=True)  33.9 us
    dot_general x6, matrix products, local(): jnp.einsum('ltp,lpq->ltq', remote_in, remote_weight, preferred_element_ty...  22.5 us
    all_to_all x1, starting transfers between devices, local(): lax.all_to_all(want_delay.reshape(devices, capacity), 'area', split_axis=...  8 us
    all_to_all x1, starting transfers between devices, local(): lax.all_to_all(want_block.reshape(devices, capacity), 'area', split_axis=...  7.35 us
  transfers between devices with their start and end apart: 8, of which 7 were waited for; matrix products, arithmetic and copies ran while one was open for 6% of the time, Pallas kernels for 0%

commit v1 on v0

v1 whole, which is shorter than its diff:
```python
import functools

import jax
import jax.numpy as jnp
from jax import lax
from jax.experimental import pallas as pl
from jax.experimental.pallas import tpu as pltpu
from jax.sharding import PartitionSpec as P

STEPS = 6
DMAX = 4
SLICES = STEPS - 2 + DMAX
UNROLL = 8
MESH = pl.DeviceIdType.MESH


def kernel(nz, ny, *refs):
    (
        history, drive, leak, inhibition, section, link_source, link_block, link_target, link_delay,
        remote_weight, local_block, local_target, local_delay, local_weight, out,
    ) = refs[:15]
    rest = refs[15:]
    gathered = rest[:SLICES]
    own = rest[SLICES : SLICES + DMAX + STEPS - 1]
    (
        w_remote, w_local, sums, area_mask, place,
        w_sem, sum_send, sum_recv, z_send, z_recv, y_send, y_recv, c_send, c_recv, d_send, d_recv,
    ) = rest[SLICES + DMAX + STEPS - 1 :]
    n = nz * ny * 2
    trials, width = drive.shape
    pop = w_remote.shape[1]
    blocks = width // pop
    links = link_block.shape[0]
    locals_ = local_block.shape[0]

    me = lax.axis_index("area")
    core = lax.rem(me, 2)
    y = lax.rem(me // 2, ny)
    z = me // (2 * ny)
    line = (y * 2 + core) * nz
    line_y = ((1 - y) * 2 + core) * nz
    my_place = line + z
    sibling = me + 1 - 2 * core
    across = me + (1 - 2 * y) * 2

    barrier = pltpu.get_barrier_semaphore()

    @pl.loop(1, n)
    def _(k):
        pl.semaphore_signal(barrier, inc=1, device_id={"area": lax.rem(me + k, n)}, device_id_type=MESH)

    load_local = pltpu.make_async_copy(local_weight, w_local, w_sem.at[0])
    load_remote = pltpu.make_async_copy(remote_weight, w_remote, w_sem.at[1])
    load_local.start()
    load_remote.start()

    def keep(s, values):
        for b in range(blocks):
            own[s][b] = values[b]
            if s < SLICES:
                gathered[s][my_place * blocks + b] = values[b]

    for s in range(DMAX):
        keep(s, [history[DMAX - 1 - s, :, b * pop : (b + 1) * pop] for b in range(blocks)])

    rows = lax.broadcasted_iota(jnp.int32, (trials, 128), 0)
    lanes = lax.broadcasted_iota(jnp.int32, (trials, 128), 1)
    diagonal = rows == lanes

    def put_sum(t, values):
        total = values[0].astype(jnp.float32)
        for b in range(1, blocks):
            total = total + values[b].astype(jnp.float32)
        column = jnp.sum(total, axis=1, keepdims=True)
        row = jnp.sum(jnp.where(diagonal, column, 0.0), axis=0, keepdims=True)
        sums[t, pl.ds(me, 1), :] = row

    def send_sums(t):
        @pl.loop(1, n)
        def _(k):
            pltpu.make_async_remote_copy(
                src_ref=sums.at[t, pl.ds(me, 1)],
                dst_ref=sums.at[t, pl.ds(me, 1)],
                send_sem=sum_send.at[t],
                recv_sem=sum_recv.at[t],
                device_id={"area": lax.rem(me + k, n)},
                device_id_type=MESH,
            ).start()

    def await_bytes(ref, sem):
        pltpu.make_async_copy(ref, ref, sem).wait()

    def part(s, start, count):
        return gathered[s].at[pl.ds(start * blocks, count * blocks)]

    def z_start(s):
        @pl.loop(1, nz)
        def _(k):
            there = lax.rem(z + k, nz)
            pltpu.make_async_remote_copy(
                src_ref=part(s, my_place, 1),
                dst_ref=part(s, my_place, 1),
                send_sem=z_send.at[s],
                recv_sem=z_recv.at[s],
                device_id={"area": (there * ny + y) * 2 + core},
                device_id_type=MESH,
            ).start()

    def relay(s, start, target, send, recv):
        return pltpu.make_async_remote_copy(
            src_ref=part(s, start, nz),
            dst_ref=part(s, start, nz),
            send_sem=send.at[s],
            recv_sem=recv.at[s],
            device_id={"area": target},
            device_id_type=MESH,
        )

    def z_done(s):
        await_bytes(part(s, line, nz - 1), z_recv.at[s])
        if ny == 2:
            relay(s, line, across, y_send, y_recv).start()
        relay(s, line, sibling, c_send, c_recv).start()

    def y_done(s):
        if ny == 2:
            await_bytes(part(s, line_y, nz), y_recv.at[s])
            relay(s, line_y, sibling, d_send, d_recv).start()

    def c_done(s):
        await_bytes(part(s, line, nz), c_recv.at[s])
        if ny == 2:
            await_bytes(part(s, line_y, nz), d_recv.at[s])

    put_sum(0, [own[DMAX - 1][b] for b in range(blocks)])
    pl.semaphore_wait(barrier, n - 1)
    send_sums(0)
    for s in range(DMAX):
        z_start(s)

    @pl.loop(0, links)
    def _(l):
        q = link_source[l]
        at = (lax.rem(q // 2, ny) * 2 + lax.rem(q, 2)) * nz + q // (2 * ny)
        place[l] = at * blocks + link_block[l]

    my_area = section[me]
    count = jnp.float32(0.0)
    for q in range(n):
        same = jnp.where(section[q] == my_area, 1.0, 0.0).astype(jnp.float32)
        count = count + same
        area_mask[q : q + 1, :] = jnp.full((1, 128), same, jnp.float32)
    inhibit = inhibition[my_area]
    neurons = jnp.full((1, 128), count * float(width), jnp.float32)

    zero = jnp.zeros((trials, pop), jnp.bfloat16)

    def dots(acc, total, sources, first, at_ref, delay_ref, target_ref, weight):
        def body(g, acc):
            columns = []
            for u in range(UNROLL):
                l = g * UNROLL + u
                at, delay, target = at_ref[l], delay_ref[l], target_ref[l]
                x = sources[-1][at]
                for i in range(len(sources) - 2, -1, -1):
                    x = lax.select(delay == first + i, sources[i][at], x)
                columns.append(jnp.concatenate([lax.select(target == b, x, zero) for b in range(blocks)], axis=0))
            lhs = jnp.concatenate(columns, axis=1)
            w = weight[pl.ds(g * UNROLL, UNROLL)].reshape(UNROLL * pop, pop)
            return acc + jnp.dot(lhs, w, preferred_element_type=jnp.float32)

        return lax.fori_loop(0, total // UNROLL, body, acc)

    def local_dots(t, acc):
        return dots(
            acc, locals_, [own[t + DMAX - d] for d in range(1, DMAX + 1)], 1, local_block, local_delay, local_target, w_local
        )

    def remote_dots(t, acc):
        return dots(
            acc, links, [gathered[t + DMAX - d] for d in range(2, DMAX + 1)], 2, place, link_delay, link_target, w_remote
        )

    def finish(t, acc):
        await_bytes(sums.at[t, pl.ds(0, n - 1)], sum_recv.at[t])
        total = jnp.sum(sums[t] * area_mask[...], axis=0, keepdims=True)
        row = inhibit * (total / neurons)
        held = jnp.sum(jnp.where(diagonal, row, 0.0), axis=1, keepdims=True)
        fresh = []
        for b in range(blocks):
            cut = slice(b * pop, (b + 1) * pop)
            gain = leak[:, cut]
            pushed = acc[b * trials : (b + 1) * trials] + drive[:, cut].astype(jnp.float32) - held
            previous = own[t + DMAX - 1][b].astype(jnp.float32)
            fresh.append(((1.0 - gain) * previous + gain * jax.nn.sigmoid(pushed)).astype(jnp.bfloat16))
        return fresh

    for t in range(STEPS):
        acc = jnp.zeros((blocks * trials, pop), jnp.float32)
        if t == 0:
            load_local.wait()
            acc = local_dots(t, acc)
            z_done(0)
            z_done(1)
            y_done(0)
            z_done(2)
            y_done(1)
            z_done(3)
            y_done(2)
            load_remote.wait()
            for s in range(DMAX - 1):
                c_done(s)
            acc = remote_dots(t, acc)
            y_done(3)
        else:
            if t >= 2:
                y_done(t + DMAX - 2)
            acc = local_dots(t, acc)
            c_done(t + DMAX - 2)
            acc = remote_dots(t, acc)
            if t + DMAX - 1 < SLICES:
                z_done(t + DMAX - 1)
        fresh = finish(t, acc)
        if t == STEPS - 1:
            for b in range(blocks):
                out[:, b * pop : (b + 1) * pop] = fresh[b]
        else:
            keep(t + DMAX, fresh)
            put_sum(t + 1, fresh)
            send_sums(t + 1)
            if t + DMAX < SLICES:
                z_start(t + DMAX)

    for t in range(STEPS):
        await_bytes(sums.at[t, pl.ds(0, n - 1)], sum_send.at[t])
    for s in range(SLICES):
        await_bytes(part(s, line, nz - 1), z_send.at[s])
        await_bytes(part(s, line, nz), c_send.at[s])
        if ny == 2:
            await_bytes(part(s, line, nz), y_send.at[s])
            await_bytes(part(s, line_y, nz), d_send.at[s])


def local(nz, ny, *args):
    (history, drive, leak, inhibition, section, link_source, *others) = args
    remote_weight, local_weight = others[3], others[7]
    depth, trials, width = history.shape
    pop = remote_weight.shape[1]
    blocks = width // pop
    n = nz * ny * 2
    vmem, smem, hbm = (
        pl.BlockSpec(memory_space=pltpu.VMEM),
        pl.BlockSpec(memory_space=pltpu.SMEM),
        pl.BlockSpec(memory_space=pl.ANY),
    )
    dma = pltpu.SemaphoreType.DMA
    return pl.pallas_call(
        functools.partial(kernel, nz, ny),
        out_shape=jax.ShapeDtypeStruct((trials, width), jnp.bfloat16),
        in_specs=[vmem, vmem, vmem, smem, smem, smem, smem, smem, smem, hbm, smem, smem, smem, hbm],
        out_specs=vmem,
        scratch_shapes=[
            *[pltpu.VMEM((n * blocks, trials, pop), jnp.bfloat16) for _ in range(SLICES)],
            *[pltpu.VMEM((blocks, trials, pop), jnp.bfloat16) for _ in range(DMAX + STEPS - 1)],
            pltpu.VMEM(remote_weight.shape, jnp.bfloat16),
            pltpu.VMEM(local_weight.shape, jnp.bfloat16),
            pltpu.VMEM((STEPS, n, 128), jnp.float32),
            pltpu.VMEM((n, 128), jnp.float32),
            pltpu.SMEM((link_source.shape[0],), jnp.int32),
            dma((2,)),
            dma((STEPS,)),
            dma((STEPS,)),
            *[dma((SLICES,)) for _ in range(8)],
        ],
        compiler_params=pltpu.CompilerParams(
            collective_id=0, has_side_effects=True, vmem_limit_bytes=52 * 1024 * 1024
        ),
    )(history, drive, leak.reshape(1, -1), inhibition, section, link_source.reshape(-1), *others)


def solution(mesh):
    ny = 2 if mesh.shape["runs"] == 2 else 1
    nz = mesh.shape["area"] // (2 * ny)
    placed = (
        P(None, "runs", "area"),
        P("runs", "area"),
        P(("runs", "area")),
        P("runs"),
        P(),
        P("area", None),
        P("area"),
        P("area"),
        P("area"),
        P(("runs", "area"), None, None),
        P("area"),
        P("area"),
        P("area"),
        P(("runs", "area"), None, None),
    )
    return jax.shard_map(
        functools.partial(local, nz, ny), mesh=mesh, in_specs=placed, out_specs=P("runs", "area"), check_vma=False
    )
```

time: 363 us -> 71.7 us (0.20)
  blocking collectives: 175 us -> 0 us
  waiting for transfers between devices: 66.6 us -> 0 us
  Pallas kernels: 0 us -> 62.5 us
  starting transfers between devices: 49.2 us -> 0 us
  matrix products: 33.8 us -> 0 us
  other arithmetic: 18.7 us -> 0 us
  local copies, waits for them, and re-layouts: 16.2 us -> 8.86 us
    psum x6 -> x0, blocking collectives: 175 us -> none  [local(): summed = lax.psum(area_table, 'area')]
    all_to_all x8 -> x0, waiting for transfers between devices: 66.6 us -> none  [the longest x6 62.6 us: local(): lax.all_to_all(outgoing, 'area', split_axis=0, concat_axis=0, tiled=True)]
    pallas_call x0 -> x1, Pallas kernels: none -> 62.5 us  [local(): pl.pallas_call(functools.partial(kernel, nz, ny), out_shape=jax.ShapeDtyp...]
    all_to_all x8 -> x0, starting transfers between devices: 49.2 us -> none  [the longest x6 33.9 us: local(): lax.all_to_all(outgoing, 'area', split_axis=0, concat_axis=0, tiled=True)]
    dot_general x24 -> x0, matrix products: 33.8 us -> none  [the longest x6 22.5 us: local(): jnp.einsum('ltp,lpq->ltq', remote_in, remote_weight, preferred_element_ty...]
    gather x18 -> x0, local copies, waits for them, and re-layouts: 10.3 us -> none  [the longest x6 3.49 us: local(): jnp.take(state_rows, (asked_delay - 1) * blocks + asked_block, axis=0)]
    unnamed x7 -> x25, local copies, waits for them, and re-layouts: 0.64 us -> 8.86 us
    reduce_sum x12 -> x0, other arithmetic: 6.38 us -> none  [the longest x1 2.01 us: local(): inhibit = jnp.sum(jnp.where(area_mask, inhibition, 0.0))]
  transfers between devices with their start and end apart: 8 -> 0, of which waited for: 7 -> 0; matrix products, arithmetic and copies ran while one was open for 6% -> 0% of each run, Pallas kernels for 0% -> 0%
where the time goes in v1:
time: 71.7 us; the launch traced here: 71.4 us
  Pallas kernels  62.5 us (87%)
  local copies, waits for them, and re-layouts  8.86 us (12%)
    pallas_call x1, Pallas kernels, local(): pl.pallas_call(functools.partial(kernel, nz, ny), out_shape=jax.ShapeDtyp...  62.5 us
    unnamed x25, local copies, waits for them, and re-layouts  8.86 us

profile of v1, /device:TPU:1, one launch (start us, length us, event | category | flops | bytes accessed | tf_op | source)
XLA Modules:
  0.0 71.4 jit_solution(7229641516076044035)
XLA Ops:
  0.0 0.0 copy-start
  0.0 0.9 %copy-done = bf16[4,16,1024]{2,1,0:T(8,128)(2,1)S(1)} copy-done((bf16[4,16,1024]{2,1,0:T(8,128)(2,1)S(1)}, bf16[4,16,1024]{2,1,0:T(8,128)(2,1)}, u32[]{:S(2)}) %copy-start) | copy-done | bytes 131096
  0.9 0.0 copy-start.1
  0.9 0.8 %copy-done.1 = bf16[16,1024]{1,0:T(8,128)(2,1)S(1)} copy-done((bf16[16,1024]{1,0:T(8,128)(2,1)S(1)}, bf16[16,1024]{1,0:T(8,128)(2,1)}, u32[]{:S(2)}) %copy-start.1) | copy-done | bytes 32792
  1.7 0.0 copy-start.2
  1.7 0.7 copy-done.2
  2.4 0.0 copy-start.3
  2.4 0.7 copy-done.3
  3.0 0.0 copy-start.4
  3.0 0.7 copy-done.4
  3.7 0.0 copy-start.5
  3.7 0.7 copy-done.5
  4.3 0.0 copy-start.6
  4.3 0.7 copy-done.6
  5.0 0.0 copy-start.7
  5.0 0.7 copy-done.7
  5.6 0.0 copy-start.8
  5.6 0.7 copy-done.8
  6.3 0.0 copy-start.9
  6.3 0.7 copy-done.9
  6.9 0.0 copy-start.10
  6.9 0.7 copy-done.10
  7.6 0.0 copy-start.11
  7.6 0.7 copy-done.11
  8.3 62.5 %shard_map.136 = bf16[16,1024]{1,0:T(8,128)(2,1)S(1)} custom-call(bf16[4,16,1024]{2,1,0:T(8,128)(2,1)S(1)} %copy-done, bf16[16,1024]{1,0:T(8,128)(2,1)S(1)} %copy-done.1, f32[1,1024]{1,0:T(1,128)S(1)} %bitcast.2, f32[8]{0:T(128)S(1)} %copy-done.3, s32[16]{0:T(128)S(1)} %copy-done.4, s32[48]{0:T(128)S(1)} %bitcast.3, s32[48]{0:T(128)S(1)} %copy-done.6, ...), custom_call_target="tpu_custom_call" | custom-call | tf_op jit(solution)/shard_map/pallas_call | solution.py:257
  70.8 0.6 copy.16
Async XLA Ops:
  0.0 0.9 %copy-start = (bf16[4,16,1024]{2,1,0:T(8,128)(2,1)S(1)}, bf16[4,16,1024]{2,1,0:T(8,128)(2,1)}, u32[]{:S(2)}) copy-start(bf16[4,16,1024]{2,1,0:T(8,128)(2,1)} %refs_0_.1) | copy-start | bytes 393220
  0.9 0.8 %copy-start.1 = (bf16[16,1024]{1,0:T(8,128)(2,1)S(1)}, bf16[16,1024]{1,0:T(8,128)(2,1)}, u32[]{:S(2)}) copy-start(bf16[16,1024]{1,0:T(8,128)(2,1)} %refs_1_.1) | copy-start | bytes 98308
  1.7 0.7 copy-start.2
  2.4 0.7 copy-start.3
  3.0 0.7 copy-start.4
  3.7 0.7 copy-start.5
  4.3 0.7 copy-start.6
  5.0 0.7 copy-start.7
  5.6 0.7 copy-start.8
  6.3 0.7 copy-start.9
  6.9 0.7 copy-start.10
  7.6 0.7 copy-start.11

commit v2 on v1

--- a/solution.py
+++ b/solution.py
@@ -9,22 +9,27 @@
 
 STEPS = 6
 DMAX = 4
+MOST_SEC = 6
 SLICES = STEPS - 2 + DMAX
-UNROLL = 8
+UNROLL = 16
 MESH = pl.DeviceIdType.MESH
 
 
 def kernel(nz, ny, *refs):
+    remote_weight, local_weight = refs[9], refs[13]
+    small = [*refs[:9], *refs[10:13]]
+    out = refs[14]
+    held_small = refs[15 : 15 + len(small)]
     (
         history, drive, leak, inhibition, section, link_source, link_block, link_target, link_delay,
-        remote_weight, local_block, local_target, local_delay, local_weight, out,
-    ) = refs[:15]
-    rest = refs[15:]
+        local_block, local_target, local_delay,
+    ) = held_small
+    rest = refs[15 + len(small) :]
     gathered = rest[:SLICES]
     own = rest[SLICES : SLICES + DMAX + STEPS - 1]
     (
         w_remote, w_local, sums, area_mask, place,
-        w_sem, sum_send, sum_recv, z_send, z_recv, y_send, y_recv, c_send, c_recv, d_send, d_recv,
+        in_sem, w_sem, sum_send, sum_recv, z_send, z_recv, y_send, y_recv, c_send, c_recv, d_send, d_recv,
     ) = rest[SLICES + DMAX + STEPS - 1 :]
     n = nz * ny * 2
     trials, width = drive.shape
@@ -43,12 +48,17 @@
     sibling = me + 1 - 2 * core
     across = me + (1 - 2 * y) * 2
 
+    sums[...] = jnp.zeros_like(sums)
+
     barrier = pltpu.get_barrier_semaphore()
 
     @pl.loop(1, n)
     def _(k):
         pl.semaphore_signal(barrier, inc=1, device_id={"area": lax.rem(me + k, n)}, device_id_type=MESH)
 
+    loads = [pltpu.make_async_copy(a, b, in_sem.at[i]) for i, (a, b) in enumerate(zip(small, held_small))]
+    for load in loads:
+        load.start()
     load_local = pltpu.make_async_copy(local_weight, w_local, w_sem.at[0])
     load_remote = pltpu.make_async_copy(remote_weight, w_remote, w_sem.at[1])
     load_local.start()
@@ -60,6 +70,7 @@
             if s < SLICES:
                 gathered[s][my_place * blocks + b] = values[b]
 
+    loads[0].wait()
     for s in range(DMAX):
         keep(s, [history[DMAX - 1 - s, :, b * pop : (b + 1) * pop] for b in range(blocks)])
 
@@ -75,17 +86,28 @@
         row = jnp.sum(jnp.where(diagonal, column, 0.0), axis=0, keepdims=True)
         sums[t, pl.ds(me, 1), :] = row
 
+    def each_mate(act):
+        for i, k in enumerate(k for m in range(1, MOST_SEC) for k in (m, -m)):
+
+            @pl.when((me + k >= 0) & (me + k < n))
+            def _(i=i, k=k):
+                act(i, k)
+
+    def sum_copy(t, i, k):
+        return pltpu.make_async_remote_copy(
+            src_ref=sums.at[t, pl.ds(me, 1)],
+            dst_ref=sums.at[t, pl.ds(me, 1)],
+            send_sem=sum_send.at[t, i],
+            recv_sem=sum_recv.at[t, i],
+            device_id={"area": me + k},
+            device_id_type=MESH,
+        )
+
     def send_sums(t):
-        @pl.loop(1, n)
-        def _(k):
-            pltpu.make_async_remote_copy(
-                src_ref=sums.at[t, pl.ds(me, 1)],
-                dst_ref=sums.at[t, pl.ds(me, 1)],
-                send_sem=sum_send.at[t],
-                recv_sem=sum_recv.at[t],
-                device_id={"area": lax.rem(me + k, n)},
-                device_id_type=MESH,
-            ).start()
+        each_mate(lambda i, k: sum_copy(t, i, k).start())
+
+    def await_sums(t):
+        each_mate(lambda i, k: await_bytes(sums.at[t, pl.ds(me + k, 1)], sum_recv.at[t, i ^ 1]))
 
     def await_bytes(ref, sem):
         pltpu.make_async_copy(ref, ref, sem).wait()
@@ -93,39 +115,52 @@
     def part(s, start, count):
         return gathered[s].at[pl.ds(start * blocks, count * blocks)]
 
-    def z_start(s):
-        @pl.loop(1, nz)
-        def _(k):
-            there = lax.rem(z + k, nz)
-            pltpu.make_async_remote_copy(
-                src_ref=part(s, my_place, 1),
-                dst_ref=part(s, my_place, 1),
-                send_sem=z_send.at[s],
-                recv_sem=z_recv.at[s],
-                device_id={"area": (there * ny + y) * 2 + core},
-                device_id_type=MESH,
-            ).start()
-
-    def relay(s, start, target, send, recv):
+    def xor(k):
+        return sum((1 << b) * (1 - 2 * lax.rem(z // (1 << b), 2)) for b in range(2) if k >> b & 1) + z
+
+    def each_other(act):
+        if nz == 4:
+            for k in range(1, nz):
+                act(k, xor(k), xor(k))
+        else:
+
+            @pl.loop(1, nz)
+            def _(k):
+                act(k, lax.rem(z + k, nz), lax.rem(z + nz - k, nz))
+
+    def copy(s, start, count, target, send, recv):
         return pltpu.make_async_remote_copy(
-            src_ref=part(s, start, nz),
-            dst_ref=part(s, start, nz),
-            send_sem=send.at[s],
-            recv_sem=recv.at[s],
+            src_ref=part(s, start, count),
+            dst_ref=part(s, start, count),
+            send_sem=send,
+            recv_sem=recv,
             device_id={"area": target},
             device_id_type=MESH,
         )
 
+    def y_copy(s, start):
+        if ny == 2:
+            copy(s, start, 1, across, y_send.at[s], y_recv.at[s]).start()
+
+    def z_start(s):
+        def send(k, to, source):
+            copy(s, my_place, 1, (to * ny + y) * 2 + core, z_send.at[s], z_recv.at[s, k]).start()
+
+        each_other(send)
+        y_copy(s, my_place)
+
     def z_done(s):
-        await_bytes(part(s, line, nz - 1), z_recv.at[s])
-        if ny == 2:
-            relay(s, line, across, y_send, y_recv).start()
-        relay(s, line, sibling, c_send, c_recv).start()
+        def forward(k, to, source):
+            await_bytes(part(s, line + source, 1), z_recv.at[s, k])
+            y_copy(s, line + source)
+
+        each_other(forward)
+        copy(s, line, nz, sibling, c_send.at[s], c_recv.at[s]).start()
 
     def y_done(s):
         if ny == 2:
             await_bytes(part(s, line_y, nz), y_recv.at[s])
-            relay(s, line_y, sibling, d_send, d_recv).start()
+            copy(s, line_y, nz, sibling, d_send.at[s], d_recv.at[s]).start()
 
     def c_done(s):
         await_bytes(part(s, line, nz), c_recv.at[s])
@@ -137,6 +172,9 @@
     send_sums(0)
     for s in range(DMAX):
         z_start(s)
+
+    for load in loads[1:]:
+        load.wait()
 
     @pl.loop(0, links)
     def _(l):
@@ -182,7 +220,7 @@
         )
 
     def finish(t, acc):
-        await_bytes(sums.at[t, pl.ds(0, n - 1)], sum_recv.at[t])
+        await_sums(t)
         total = jnp.sum(sums[t] * area_mask[...], axis=0, keepdims=True)
         row = inhibit * (total / neurons)
         held = jnp.sum(jnp.where(diagonal, row, 0.0), axis=1, keepdims=True)
@@ -213,13 +251,13 @@
             acc = remote_dots(t, acc)
             y_done(3)
         else:
+            acc = local_dots(t, acc)
             if t >= 2:
                 y_done(t + DMAX - 2)
-            acc = local_dots(t, acc)
             c_done(t + DMAX - 2)
-            acc = remote_dots(t, acc)
             if t + DMAX - 1 < SLICES:
                 z_done(t + DMAX - 1)
+            acc = remote_dots(t, acc)
         fresh = finish(t, acc)
         if t == STEPS - 1:
             for b in range(blocks):
@@ -232,7 +270,7 @@
                 z_start(t + DMAX)
 
     for t in range(STEPS):
-        await_bytes(sums.at[t, pl.ds(0, n - 1)], sum_send.at[t])
+        each_mate(lambda i, k: sum_copy(t, i, k).wait_send())
     for s in range(SLICES):
         await_bytes(part(s, line, nz - 1), z_send.at[s])
         await_bytes(part(s, line, nz), c_send.at[s])
@@ -248,18 +286,17 @@
     pop = remote_weight.shape[1]
     blocks = width // pop
     n = nz * ny * 2
-    vmem, smem, hbm = (
-        pl.BlockSpec(memory_space=pltpu.VMEM),
-        pl.BlockSpec(memory_space=pltpu.SMEM),
-        pl.BlockSpec(memory_space=pl.ANY),
-    )
+    operands = [history, drive, leak.reshape(1, -1), inhibition, section, link_source.reshape(-1), *others]
+    small = [*operands[:9], *operands[10:13]]
     dma = pltpu.SemaphoreType.DMA
     return pl.pallas_call(
         functools.partial(kernel, nz, ny),
         out_shape=jax.ShapeDtypeStruct((trials, width), jnp.bfloat16),
-        in_specs=[vmem, vmem, vmem, smem, smem, smem, smem, smem, smem, hbm, smem, smem, smem, hbm],
-        out_specs=vmem,
+        in_specs=[pl.BlockSpec(memory_space=pltpu.HBM)] * len(operands),
+        out_specs=pl.BlockSpec(memory_space=pltpu.VMEM),
         scratch_shapes=[
+            *[pltpu.VMEM(a.shape, a.dtype) for a in small[:3]],
+            *[pltpu.SMEM(a.shape, a.dtype) for a in small[3:]],
             *[pltpu.VMEM((n * blocks, trials, pop), jnp.bfloat16) for _ in range(SLICES)],
             *[pltpu.VMEM((blocks, trials, pop), jnp.bfloat16) for _ in range(DMAX + STEPS - 1)],
             pltpu.VMEM(remote_weight.shape, jnp.bfloat16),
@@ -267,15 +304,18 @@
             pltpu.VMEM((STEPS, n, 128), jnp.float32),
             pltpu.VMEM((n, 128), jnp.float32),
             pltpu.SMEM((link_source.shape[0],), jnp.int32),
+            dma((len(small),)),
             dma((2,)),
-            dma((STEPS,)),
-            dma((STEPS,)),
-            *[dma((SLICES,)) for _ in range(8)],
+            dma((STEPS, 2 * (MOST_SEC - 1))),
+            dma((STEPS, 2 * (MOST_SEC - 1))),
+            dma((SLICES,)),
+            dma((SLICES, nz)),
+            *[dma((SLICES,)) for _ in range(6)],
         ],
         compiler_params=pltpu.CompilerParams(
-            collective_id=0, has_side_effects=True, vmem_limit_bytes=52 * 1024 * 1024
+            collective_id=0, has_side_effects=True, vmem_limit_bytes=60 * 1024 * 1024
         ),
-    )(history, drive, leak.reshape(1, -1), inhibition, section, link_source.reshape(-1), *others)
+    )(*operands)
 
 
 def solution(mesh):

time: 71.7 us -> 57.2 us (0.80)
  local copies, waits for them, and re-layouts: 8.86 us -> 1.38 us
  Pallas kernels: 62.5 us -> 55.6 us
    unnamed x25 -> x1, local copies, waits for them, and re-layouts: 8.86 us -> 1.38 us
    pallas_call x1, Pallas kernels: 62.5 us -> 55.6 us  [local(): pl.pallas_call(functools.partial(kernel, nz, ny), out_shape=jax.ShapeDtyp...]
where the time goes in v2:
time: 57.2 us; the launch traced here: 57 us
  Pallas kernels  55.6 us (97%)
  local copies, waits for them, and re-layouts  1.38 us (2%)
    pallas_call x1, Pallas kernels, local(): pl.pallas_call(functools.partial(kernel, nz, ny), out_shape=jax.ShapeDtyp...  55.6 us
    unnamed x1, local copies, waits for them, and re-layouts  1.38 us

profile of v2, /device:TPU:1, one launch (start us, length us, event | category | flops | bytes accessed | tf_op | source)
XLA Modules:
  0.0 57.0 jit_solution(1010042041189906947)
XLA Ops:
  0.0 55.6 %shard_map.136 = bf16[16,1024]{1,0:T(8,128)(2,1)} custom-call(bf16[4,16,1024]{2,1,0:T(8,128)(2,1)} %refs_0_.1, bf16[16,1024]{1,0:T(8,128)(2,1)} %refs_1_.1, f32[1,1024]{1,0:T(1,128)} %bitcast.2, f32[8]{0:T(128)} %refs_3_.1, s32[16]{0:T(128)} %refs_4_.1, s32[48]{0:T(128)} %bitcast.3, s32[48]{0:T(128)} %refs_6_.1, s32[48]{0:T(128)} %refs_7_.1, s32[48]{0:T(128)} %refs_8_.1, ...), custom_call_target="tpu_custom_call" | custom-call | tf_op jit(solution)/shard_map/pallas_call | solution.py:292
  55.6 1.4 %copy.16 = bf16[16,1024]{1,0:T(8,128)(2,1)} copy(bf16[16,1024]{1,0:T(8,128)(2,1)} %shard_map.136) | data formatting | bytes 65536

commit v3 on v2

--- a/solution.py
+++ b/solution.py
@@ -243,17 +243,15 @@
             y_done(0)
             z_done(2)
             y_done(1)
-            z_done(3)
             y_done(2)
             load_remote.wait()
             for s in range(DMAX - 1):
                 c_done(s)
             acc = remote_dots(t, acc)
-            y_done(3)
+            z_done(3)
         else:
             acc = local_dots(t, acc)
-            if t >= 2:
-                y_done(t + DMAX - 2)
+            y_done(t + DMAX - 2)
             c_done(t + DMAX - 2)
             if t + DMAX - 1 < SLICES:
                 z_done(t + DMAX - 1)

time: 57.2 us -> 56.4 us (0.986)
  Pallas kernels: 55.6 us -> 54.9 us
    pallas_call x1, Pallas kernels: 55.6 us -> 54.9 us  [local(): pl.pallas_call(functools.partial(kernel, nz, ny), out_shape=jax.ShapeDtyp...]
where the time goes in v3:
time: 56.4 us; the launch traced here: 56.3 us
  Pallas kernels  54.9 us (97%)
  local copies, waits for them, and re-layouts  1.38 us (2%)
    pallas_call x1, Pallas kernels, local(): pl.pallas_call(functools.partial(kernel, nz, ny), out_shape=jax.ShapeDtyp...  54.9 us
    unnamed x1, local copies, waits for them, and re-layouts  1.38 us

profile of v3, /device:TPU:1, one launch (start us, length us, event | category | flops | bytes accessed | tf_op | source)
XLA Modules:
  0.0 56.3 jit_solution(4630946937579789462)
XLA Ops:
  0.0 54.9 %shard_map.136 = bf16[16,1024]{1,0:T(8,128)(2,1)} custom-call(bf16[4,16,1024]{2,1,0:T(8,128)(2,1)} %refs_0_.1, bf16[16,1024]{1,0:T(8,128)(2,1)} %refs_1_.1, f32[1,1024]{1,0:T(1,128)} %bitcast.2, f32[8]{0:T(128)} %refs_3_.1, s32[16]{0:T(128)} %refs_4_.1, s32[48]{0:T(128)} %bitcast.3, s32[48]{0:T(128)} %refs_6_.1, s32[48]{0:T(128)} %refs_7_.1, s32[48]{0:T(128)} %refs_8_.1, ...), custom_call_target="tpu_custom_call" | custom-call | tf_op jit(solution)/shard_map/pallas_call | solution.py:290
  54.9 1.4 %copy.16 = bf16[16,1024]{1,0:T(8,128)(2,1)} copy(bf16[16,1024]{1,0:T(8,128)(2,1)} %shard_map.136) | data formatting | bytes 65536
